TPU v7x, 32 devices: a whole 2x2x4 slice. The times are simulated.
32 devices in a mesh: dp: 16 (over z, y, core), mp: 2 (over x).
Axes of the slice: x: 2, y: 2, z: 4, core: 2. Of those that a mesh axis runs over, the one named last changes fastest.
Arguments:
- context: bfloat16 [16384, 2048], P('dp', 'mp'), may hold values from -6 to 6
- cotangent: bfloat16 [16384, 4096], P(('dp', 'mp')), may hold values from -6 to 6
- lengths: int32 [512], P(('dp', 'mp')), may hold values from 1 to 32, as said below
- weight: float32 [2048, 4096], P('mp', 'dp'), may hold values from -0.125 to 0.125
- row_stat: float32 [2048], P('mp'), may hold values from 0.01 to 0.3
- col_stat: float32 [4096], P('dp'), may hold values from 0.01 to 0.3
Outputs:
- context_grad: bfloat16 [16384, 2048], P('dp', 'mp')
- update: float32 [2048, 4096], P('mp', 'dp')
- row_new: float32 [2048], P('mp')
- col_new: float32 [4096], P('dp')
Inputs may be any that keep to these rules, and one draw needn't show every extreme that they name: The first lengths entry of each sequence's 32 slots are real tokens, the rest padding.
All inputs are finite; a program needn't handle non-finite values.
Results may differ from a plain program's by a relative error of at most 0.0049.
Values may be sent and summed in bfloat16 or wider, within the bound.
A program may use at most 128 MiB of HBM per device.

v0:
```python
import jax
import jax.numpy as jnp
from jax import lax
from jax.sharding import PartitionSpec as P

decay_rate = 0.9
square_eps = 1e-30


def per_device(context, cotangent, lengths, weight, row_stat, col_stat):
    data_groups = lax.axis_size("dp")
    seq_here = lengths.shape[0]
    target_len = cotangent.shape[0] // seq_here
    model_width = cotangent.shape[1]
    position = jnp.arange(target_len, dtype=jnp.int32)
    inside = position[None, :] < lengths[:, None]
    shaped = cotangent.reshape(seq_here, target_len, model_width)
    masked = jnp.where(inside[:, :, None], shaped, jnp.zeros((), cotangent.dtype)).reshape(
        -1, model_width
    )
    weight_b = weight.astype(jnp.bfloat16)
    head_cols = context.shape[1]
    gathered = lax.all_gather(masked, "mp", axis=0, tiled=True)
    back_ctx = lax.dot_general(
        gathered,
        lax.all_gather(weight_b, "dp", axis=1, tiled=True),
        (((1,), (1,)), ((), ())),
        preferred_element_type=jnp.float32,
    )
    grad_term = lax.dot_general(
        context, gathered, (((0,), (0,)), ((), ())), preferred_element_type=jnp.float32
    )
    context_grad = back_ctx.astype(jnp.bfloat16)
    grad = lax.psum_scatter(grad_term, "dp", scatter_dimension=1, tiled=True) / data_groups
    square = grad * grad + square_eps
    inner_total = head_cols * lax.axis_size("mp")
    row_all = lax.psum(jnp.sum(square, axis=1), "dp")
    row_new = decay_rate * row_stat + (1.0 - decay_rate) * (row_all / model_width)
    col_all = lax.psum(jnp.sum(square, axis=0), "mp")
    col_new = decay_rate * col_stat + (1.0 - decay_rate) * (col_all / inner_total)
    raw_update = grad / jnp.sqrt(row_new[:, None] * col_new[None, :])
    square_sum = lax.psum(jnp.sum(raw_update * raw_update), ("dp", "mp"))
    update_rms = jnp.sqrt(square_sum / (inner_total * model_width))
    update = raw_update / jnp.maximum(1.0, update_rms)
    return (context_grad, update, row_new, col_new)


def solution(mesh):
    in_specs = (
        P("dp", "mp"),
        P(("dp", "mp"), None),
        P(("dp", "mp")),
        P("mp", "dp"),
        P("mp"),
        P("dp"),
    )
    out_specs = (P("dp", "mp"), P("mp", "dp"), P("mp"), P("dp"))
    return jax.shard_map(
        per_device, mesh=mesh, in_specs=in_specs, out_specs=out_specs, check_vma=False
    )
```

profile of v0, /device:TPU:0, one launch (start us, length us, event | category | flops | bytes accessed | tf_op | source)
XLA Modules:
  0.0 457.2 jit_solution(2788150589154650559)
XLA Ops:
  7.2 0.0 copy-start
  7.2 0.0 all-gather.3.cloned.1.call-start
  7.2 0.9 iota_compare_fusion
  8.1 0.1 lt.23
  8.2 4.5 broadcast_select_fusion
  12.6 0.0 all-gather.3.cloned.1.call-update
  12.7 0.0 reduce-scatter.2.cloned.1.call-start
  12.7 106.8 %all-gather.3.cloned.1.call-done = bf16[1024,4096]{1,0:T(8,128)(2,1)} async-done(((bf16[512,4096]{1,0:T(8,128)(2,1)}), bf16[1024,4096]{1,0:T(8,128)(2,1)}) %all-gather.3.cloned.1.call-update) | async-done | bytes 8388624 | tf_op jit(solution)/shard_map/all_gather | solution.py:23
  119.5 0.0 copy-done
  119.5 14.6 %convolution_bitcast_fusion = f32[1024,4096]{0,1:T(8,128)} fusion(bf16[1024,4096]{1,0:T(8,128)(2,1)} %all-gather.3.cloned.1.call-done, bf16[1024,1024]{1,0:T(8,128)(2,1)S(1)} %copy-done), kind=kOutput, calls=%fused_computation | convolution fusion | flops 8589934592 | bytes 27262976 | tf_op jit(solution)/shard_map/dot_general | solution.py:30
  134.1 0.0 copy-start.2
  134.1 0.0 copy-start.6
  134.1 0.0 copy-start.5
  134.1 0.0 reduce-scatter.2.cloned.1.call-update
  134.1 0.0 all-gather.5.cloned.1.call-start
  134.2 1.1 copy-done.2
  135.3 0.8 convert_element_type.6
  136.2 0.0 all-gather.5.cloned.1.call-update
  136.2 176.6 %reduce-scatter.2.cloned.1.call-done = f32[1024,256]{0,1:T(8,128)} async-done(((f32[1024,4096]{0,1:T(8,128)}), f32[1024,256]{0,1:T(8,128)}) %reduce-scatter.2.cloned.1.call-update) | async-done | bytes 1048592 | tf_op jit(solution)/shard_map/reduce_scatter | solution.py:34
  312.8 1.5 fusion.1
  314.3 4.9 %psum.22 = f32[256]{0:T(256)S(1)} all-reduce(f32[256]{0:T(256)S(1)} %get-tuple-element.9), channel_id=1, replica_groups=mesh['dp'=16,'mp'=2] {'mp'}, use_global_device_ids=true, to_apply=%region_4.5 | all-reduce | flops 256 | bytes 2048 | tf_op jit(solution)/shard_map/psum | solution.py:39
  319.2 31.0 %psum.21 = f32[1024]{0:T(1024)S(1)} all-reduce(f32[1024]{0:T(1024)S(1)} %get-tuple-element.8), channel_id=1, replica_groups=mesh['dp'=16,'mp'=2] {'dp'}, use_global_device_ids=true, to_apply=%region_2.3 | all-reduce | flops 1024 | bytes 8192 | tf_op jit(solution)/shard_map/psum | solution.py:37
  350.2 0.0 copy-done.6
  350.3 0.0 copy-done.5
  350.3 0.0 copy-start.4
  350.3 0.0 copy-start.3
  350.3 2.3 multiply_reduce_fusion
  352.6 0.0 copy-start.1
  352.6 40.2 %all-gather.5.cloned.1.call-done = bf16[1024,4096]{1,0:T(8,128)(2,1)} async-done(((bf16[1024,256]{1,0:T(8,128)(2,1)}), bf16[1024,4096]{1,0:T(8,128)(2,1)}) %all-gather.5.cloned.1.call-update) | async-done | bytes 8388624 | tf_op jit(solution)/shard_map/all_gather | solution.py:26
  392.8 14.7 %convolution_convert_fusion = bf16[1024,1024]{1,0:T(8,128)(2,1)} fusion(bf16[1024,4096]{1,0:T(8,128)(2,1)} %all-gather.3.cloned.1.call-done, bf16[1024,4096]{1,0:T(8,128)(2,1)} %all-gather.5.cloned.1.call-done), kind=kOutput, calls=%fused_computation.2 | convolution fusion | flops 8590983168 | bytes 18874368 | tf_op jit(solution)/shard_map/dot_general | solution.py:24
  407.5 38.6 %psum.23 = f32[]{:T(128)} all-reduce(f32[]{:T(128)} %multiply_reduce_fusion), channel_id=1, replica_groups=mesh['dp'=16,'mp'=2] {'dp','mp'}, use_global_device_ids=true, to_apply=%region_6.7 | all-reduce | flops 1 | bytes 8 | tf_op jit(solution)/shard_map/psum | solution.py:42
  446.8 0.0 copy-done.4
  446.8 0.0 copy-done.3
  446.9 0.0 copy-done.1
  446.9 1.3 fusion.2
  448.1 2.5 copy.10
  (2 shorter events, 0.0 us)
Async XLA Ops:
  7.2 112.4 %copy-start = (bf16[1024,1024]{1,0:T(8,128)(2,1)S(1)}, bf16[1024,1024]{1,0:T(8,128)(2,1)}, u32[]{:S(2)}) copy-start(bf16[1024,1024]{1,0:T(8,128)(2,1)} %param.6) | copy-start | bytes 6291460
  7.2 112.3 %all-gather.3.cloned.1.call-start = ((), (), s32[]{:S(2)}) async-start(), calls=%async_computation.1 | async-start | bytes 12582912 | tf_op jit(solution)/shard_map/all_gather | solution.py:23
  12.7 300.1 %reduce-scatter.2.cloned.1.call-start = ((), (), s32[]{:S(2)}) async-start(), calls=%async_computation.3 | async-start | bytes 17825792 | tf_op jit(solution)/shard_map/reduce_scatter | solution.py:34
  134.1 1.2 copy-start.2
  134.1 216.2 %copy-start.6 = (f32[256]{0:T(256)S(1)}, f32[256]{0:T(256)}, u32[]{:S(2)}) copy-start(f32[256]{0:T(256)} %param.11) | copy-start | bytes 3076
  134.1 216.2 %copy-start.5 = (f32[1024]{0:T(1024)S(1)}, f32[1024]{0:T(1024)}, u32[]{:S(2)}) copy-start(f32[1024]{0:T(1024)} %param.10) | copy-start | bytes 12292
  134.1 258.7 %all-gather.5.cloned.1.call-start = ((), (), s32[]{:S(2)}) async-start(), calls=%async_computation.2 | async-start | bytes 8912896 | tf_op jit(solution)/shard_map/all_gather | solution.py:26
  350.3 96.6 %copy-start.4 = (f32[256]{0:T(256)}, f32[256]{0:T(256)S(1)}, u32[]{:S(2)}) copy-start(f32[256]{0:T(256)S(1)} %multiply_add_fusion.2) | copy-start | bytes 3076
  350.3 96.6 %copy-start.3 = (f32[1024]{0:T(1024)}, f32[1024]{0:T(1024)S(1)}, u32[]{:S(2)}) copy-start(f32[1024]{0:T(1024)S(1)} %multiply_add_fusion.1) | copy-start | bytes 12292
  352.6 94.2 %copy-start.1 = (f32[1024,256]{0,1:T(8,128)S(1)}, f32[1024,256]{0,1:T(8,128)}, u32[]{:S(2)}) copy-start(f32[1024,256]{0,1:T(8,128)} %reduce-scatter.2.cloned.1.call-done) | copy-start | bytes 3145732
Sparse Core Ops, SparseCore 0:
  12.8 106.6 all-gather.2
  134.2 178.5 reduce-scatter.1
  315.5 77.2 all-gather.4
where the time goes:
time: 458 us; the launch traced here: 457 us
  waiting for transfers between devices  324 us (71%)
  blocking collectives  74.6 us (16%)
  matrix products  29.2 us (6%)
  between operations  14.5 us (3%)
  other arithmetic  11.2 us (2%)
    reduce_scatter x1, waiting for transfers between devices, per_device(): lax.psum_scatter(grad_term, 'dp', scatter_dimension=1, tiled=True)  177 us
    all_gather x1, waiting for transfers between devices, per_device(): gathered = lax.all_gather(masked, 'mp', axis=0, tiled=True)  107 us
    all_gather x1, waiting for transfers between devices, per_device(): lax.all_gather(weight_b, 'dp', axis=1, tiled=True)  40.2 us
    psum x1, blocking collectives, per_device(): square_sum = lax.psum(jnp.sum(raw_update * raw_update), ('dp', 'mp'))  38.6 us
    psum x1, blocking collectives, per_device(): row_all = lax.psum(jnp.sum(square, axis=1), 'dp')  31 us
    dot_general x1, matrix products, per_device(): lax.dot_general(gathered, lax.all_gather(weight_b, 'dp', axis=1, tiled=Tr...  14.7 us
    dot_general x1, matrix products, per_device(): lax.dot_general(context, gathered, (((0,), (0,)), ((), ())), preferred_el...  14.6 us
  transfers between devices with their start and end apart: 3, of which 3 were waited for; matrix products, arithmetic and copies ran while one was open for 1% of the time, Pallas kernels for 0%

commit v1 on v0

--- a/solution.py
+++ b/solution.py
@@ -1,13 +1,342 @@
+import functools
 import jax
 import jax.numpy as jnp
 from jax import lax
+from jax.experimental import pallas as pl
+from jax.experimental.pallas import tpu as pltpu
 from jax.sharding import PartitionSpec as P
 
 decay_rate = 0.9
 square_eps = 1e-30
-
-
-def per_device(context, cotangent, lengths, weight, row_stat, col_stat):
+LANES = 128
+TILE = 256
+WINDOW = 3
+MESH = pl.DeviceIdType.MESH
+
+
+def low_bit(r, n):
+    return r & -r if r else n
+
+
+def flip(me, r):
+    out = me
+    bit = 1
+    while bit <= r:
+        if r & bit:
+            out = out + bit * (1 - 2 * (lax.rem(lax.div(me, bit), 2)))
+        bit *= 2
+    return out
+
+
+def schedule(n):
+    half = n // 2
+    first = list(range(n - 2, half - 1, -2))
+    second = sorted(range(0, half, 2), key=lambda r: (low_bit(r, n), -r))
+    order = [b for r in first + second for b in (r + 1, r)]
+    pos = {r: k for k, r in enumerate(order)}
+    after = {}
+    for r in sorted(range(2, n, 2), key=lambda r: low_bit(r, n)):
+        when, bit = pos[r], 2
+        while bit < low_bit(r, n):
+            when = max(when, after[r + bit] + 3)
+            bit *= 2
+        after[r] = min(when, n - 2)
+    return order, after
+
+
+def weight_arrivals(n):
+    return sorted(range(2, n, 2), key=lambda r: (bin(r).count("1") + (n // low_bit(r, n)).bit_length(), r))
+
+
+def kernel(n, mask_ref, cot_ref, ctx_ref, w_ref, row_ref, col_ref,
+           cg_ref, up_ref, rown_ref, coln_ref,
+           ctx_t, g_all, w_all, inbox, outbox, kept, cg_acc, rv, cx, sx,
+           x_send, x_recv, w_send, w_recv, r_send, r_recv, v_send, v_recv, p_send, p_recv):
+    me, mp = lax.axis_index("dp"), lax.axis_index("mp")
+    other = 1 - mp
+    t, width = cot_ref.shape
+    heads, cols = w_ref.shape
+    groups = heads // LANES
+    own_rows = pl.ds(pl.multiple_of(mp * t, t), t)
+
+    barrier = pltpu.get_barrier_semaphore()
+    for q in range(1, n):
+        pl.semaphore_signal(barrier, inc=1, device_id=(flip(me, q), mp), device_id_type=MESH)
+    pl.semaphore_signal(barrier, inc=1, device_id=(me, other), device_id_type=MESH)
+
+    order, after = schedule(n)
+
+    def mask_block(r):
+        columns = pl.ds(pl.multiple_of(flip(me, r) * cols, cols), cols)
+        m = mask_ref[...]
+        m = jnp.concatenate([m] * (cols // LANES), axis=1)
+        g_all[r, own_rows, :] = cot_ref[:, columns] * m
+
+    w_all[0] = w_ref[...].astype(jnp.bfloat16)
+    for r in order[:WINDOW]:
+        mask_block(r)
+    pl.semaphore_wait(barrier, n)
+
+    x_copy = {}
+    for r in order:
+        x_copy[r] = pltpu.make_async_remote_copy(
+            src_ref=g_all.at[r, own_rows, :], dst_ref=g_all.at[r, own_rows, :],
+            send_sem=x_send.at[r], recv_sem=x_recv.at[r],
+            device_id=(me, other), device_id_type=MESH)
+    x_in = {
+        r: pltpu.make_async_remote_copy(
+            src_ref=g_all.at[r, own_rows, :],
+            dst_ref=g_all.at[r, pl.ds(pl.multiple_of(other * t, t), t), :],
+            send_sem=x_send.at[r], recv_sem=x_recv.at[r],
+            device_id=(me, other), device_id_type=MESH)
+        for r in order
+    }
+    for r in order[:WINDOW]:
+        x_copy[r].start()
+
+    w_copies = []
+
+    def weight_send(r):
+        bit = low_bit(r, n) // 2
+        while bit >= 1:
+            copy = pltpu.make_async_remote_copy(
+                src_ref=w_all.at[r], dst_ref=w_all.at[r ^ bit],
+                send_sem=w_send.at[len(w_copies)], recv_sem=w_recv.at[r ^ bit],
+                device_id=(flip(me, bit), mp), device_id_type=MESH)
+            copy.start()
+            w_copies.append(copy)
+            bit //= 2
+
+    def weight_wait(r):
+        pltpu.make_async_remote_copy(
+            src_ref=w_all.at[0], dst_ref=w_all.at[r],
+            send_sem=w_send.at[0], recv_sem=w_recv.at[r],
+            device_id=(flip(me, 1), mp), device_id_type=MESH).wait_recv()
+
+    weight_send(0)
+    for r in order[WINDOW:]:
+        mask_block(r)
+
+    tokens = 2 * t
+    for i in range(tokens // TILE):
+        for j in range(heads // TILE):
+            ctx_t[j * TILE:(j + 1) * TILE, i * TILE:(i + 1) * TILE] = ctx_ref[
+                i * TILE:(i + 1) * TILE, j * TILE:(j + 1) * TILE].T
+
+    def reduce_copy(r):
+        return pltpu.make_async_remote_copy(
+            src_ref=outbox.at[r - 1], dst_ref=inbox.at[r - 1],
+            send_sem=r_send.at[r], recv_sem=r_recv.at[r],
+            device_id=(flip(me, low_bit(r, n)), mp), device_id_type=MESH)
+
+    r_copy = {r: reduce_copy(r) for r in range(1, n)}
+
+    def weight_grad(r):
+        @pl.loop(0, heads // TILE)
+        def _(i):
+            rows = pl.ds(pl.multiple_of(i * TILE, TILE), TILE)
+            term = jnp.dot(ctx_t[rows, :], g_all[r], preferred_element_type=jnp.float32)
+            if r % 2:
+                outbox[r - 1, rows, :] = term.astype(jnp.bfloat16)
+            else:
+                kept[r // 2, rows, :] = term
+        if r % 2:
+            r_copy[r].start()
+
+    def incoming(r):
+        out, bit = [], 1
+        while bit < low_bit(r, n):
+            out.append(r + bit)
+            bit *= 2
+        return out
+
+    def pass_on(r):
+        for q in incoming(r):
+            r_copy[q].wait_recv()
+
+        @pl.loop(0, heads // TILE)
+        def _(i):
+            rows = pl.ds(pl.multiple_of(i * TILE, TILE), TILE)
+            total = kept[r // 2, rows, :]
+            for q in incoming(r):
+                total = total + inbox[q - 1, rows, :].astype(jnp.float32)
+            outbox[r - 1, rows, :] = total.astype(jnp.bfloat16)
+        r_copy[r].start()
+
+    def context_grad(blocks, first, last):
+        @pl.loop(0, tokens // TILE)
+        def _(i):
+            rows = pl.ds(pl.multiple_of(i * TILE, TILE), TILE)
+            total = None if first else cg_acc[rows, :]
+            for r in blocks:
+                term = lax.dot_general(g_all[r, rows, :], w_all[r], (((1,), (1,)), ((), ())),
+                                       preferred_element_type=jnp.float32)
+                total = term if total is None else total + term
+            if last:
+                cg_ref[rows, :] = total.astype(jnp.bfloat16)
+            else:
+                cg_acc[rows, :] = total
+
+    arrivals = weight_arrivals(n)
+    w_step = {}
+    for k, r in enumerate(arrivals):
+        w_step.setdefault(min(1 + (k * (n // 2 - 2)) // max(len(arrivals) - 1, 1), n - 1), []).append(r)
+    quarter = n // 4
+    cg_step = {n // 2 + 1: 0, n // 2 + 3: 1, 3 * n // 4 + 1: 2}
+    w_seen = set(range(0, 1))
+
+    for k, r in enumerate(order):
+        x_in[r].wait_recv()
+        if k + WINDOW < n:
+            x_copy[r].wait_send()
+            x_copy[order[k + WINDOW]].start()
+        weight_grad(r)
+        for q in w_step.get(k, []):
+            weight_wait(q)
+            w_seen.add(q)
+            weight_send(q)
+        for q in order:
+            if after.get(q) == k:
+                pass_on(q)
+        if k in cg_step:
+            blocks = order[cg_step[k] * quarter:(cg_step[k] + 1) * quarter]
+            for q in blocks:
+                if q not in w_seen:
+                    weight_wait(q)
+                    w_seen.add(q)
+            context_grad(blocks, cg_step[k] == 0, False)
+
+    for q in incoming(0):
+        r_copy[q].wait_recv()
+    col_part = jnp.zeros((1, cols), jnp.float32)
+
+    def row_sums(values, base, i):
+        folded = values[:, :LANES]
+        for c in range(LANES, cols, LANES):
+            folded = folded + values[:, c:c + LANES]
+        line = jnp.sum(folded.T, axis=0, keepdims=True)
+        for c in range(TILE // LANES):
+            at = base + i * (TILE // LANES) + c
+            rv[0, at:at + 1, :] = line[:, c * LANES:(c + 1) * LANES]
+
+    for i in range(heads // TILE):
+        rows = slice(i * TILE, (i + 1) * TILE)
+        total = kept[0, rows, :]
+        for q in incoming(0):
+            total = total + inbox[q - 1, rows, :].astype(jnp.float32)
+        grad = total / n
+        kept[0, rows, :] = grad
+        square = grad * grad + square_eps
+        col_part = col_part + jnp.sum(square, axis=0, keepdims=True)
+        row_sums(square, 0, i)
+    cx[0] = jnp.broadcast_to(col_part, (8, cols))
+    col_copy = pltpu.make_async_remote_copy(
+        src_ref=cx.at[0], dst_ref=cx.at[1], send_sem=p_send.at[0], recv_sem=p_recv.at[0],
+        device_id=(me, other), device_id_type=MESH)
+    col_copy.start()
+    last = order[3 * quarter:]
+    for q in last:
+        if q not in w_seen:
+            weight_wait(q)
+            w_seen.add(q)
+    context_grad(last[:len(last) // 2], False, False)
+    col_copy.wait_recv()
+    col_new = decay_rate * col_ref[...] + (1.0 - decay_rate) * (
+        (cx[0, 0:1, :] + cx[1, 0:1, :]) / (2 * heads))
+    coln_ref[...] = col_new
+    inv_col = 1.0 / col_new
+    for i in range(heads // TILE):
+        grad = kept[0, i * TILE:(i + 1) * TILE, :]
+        row_sums(grad * grad * inv_col, groups, i)
+    v_copy = []
+    for q in range(1, n):
+        copy = pltpu.make_async_remote_copy(
+            src_ref=rv.at[0], dst_ref=rv.at[q], send_sem=v_send.at[q], recv_sem=v_recv.at[q],
+            device_id=(flip(me, q), mp), device_id_type=MESH)
+        copy.start()
+        v_copy.append(copy)
+    context_grad(last[len(last) // 2:], False, True)
+    for copy in v_copy:
+        copy.wait_recv()
+    sums = [rv[q] for q in range(n)]
+    while len(sums) > 1:
+        sums = [sums[k] + sums[k + 1] for k in range(0, len(sums), 2)]
+    row_new = decay_rate * row_ref[...] + (1.0 - decay_rate) * (sums[0][:groups] / width)
+    rown_ref[...] = row_new
+    part = jnp.sum(jnp.sum(sums[0][groups:] / row_new, axis=0, keepdims=True), axis=1, keepdims=True)
+    sx[0] = jnp.broadcast_to(part, (8, LANES))
+    s_copy = pltpu.make_async_remote_copy(
+        src_ref=sx.at[0], dst_ref=sx.at[1], send_sem=p_send.at[1], recv_sem=p_recv.at[1],
+        device_id=(me, other), device_id_type=MESH)
+    s_copy.start()
+    root_row = 1.0 / jnp.sqrt(row_new)
+    root_col = 1.0 / jnp.sqrt(col_new)
+    s_copy.wait_recv()
+    rms = jnp.sqrt((sx[0, 0:1, :] + sx[1, 0:1, :]) / (2.0 * heads * width))
+    root_row = root_row / jnp.maximum(1.0, rms)
+    for k in range(groups):
+        factor = jnp.broadcast_to(root_row[k:k + 1, :], (LANES, LANES)).T
+        factor = jnp.concatenate([factor] * (cols // LANES), axis=1)
+        rows = slice(k * LANES, (k + 1) * LANES)
+        up_ref[rows, :] = kept[0, rows, :] * factor * root_col
+
+    for r in order[max(n - WINDOW, 0):]:
+        x_copy[r].wait_send()
+    for copy in w_copies:
+        copy.wait_send()
+    for r in range(1, n):
+        r_copy[r].wait_send()
+    col_copy.wait_send()
+    for copy in v_copy:
+        copy.wait_send()
+    s_copy.wait_send()
+
+
+def fused(n, context, cotangent, lengths, weight, row_stat, col_stat):
+    t, width = cotangent.shape
+    heads, cols = weight.shape
+    target_len = t // lengths.shape[0]
+    groups = heads // LANES
+    inside = jnp.arange(target_len, dtype=jnp.int32)[None, :] < lengths[:, None]
+    mask = jnp.broadcast_to(inside[:, :, None], (lengths.shape[0], target_len, LANES))
+    mask = mask.astype(jnp.bfloat16).reshape(t, LANES)
+    vmem = pl.BlockSpec(memory_space=pltpu.VMEM)
+    dma = pltpu.SemaphoreType.DMA
+    flops = 4 * 2 * t * heads * width
+    out = pl.pallas_call(
+        functools.partial(kernel, n),
+        out_shape=(
+            jax.ShapeDtypeStruct((2 * t, heads), jnp.bfloat16),
+            jax.ShapeDtypeStruct((heads, cols), jnp.float32),
+            jax.ShapeDtypeStruct((groups, LANES), jnp.float32),
+            jax.ShapeDtypeStruct((1, cols), jnp.float32),
+        ),
+        in_specs=[vmem] * 6,
+        out_specs=(vmem,) * 4,
+        scratch_shapes=[
+            pltpu.VMEM((heads, 2 * t), jnp.bfloat16),
+            pltpu.VMEM((n, 2 * t, cols), jnp.bfloat16),
+            pltpu.VMEM((n, heads, cols), jnp.bfloat16),
+            pltpu.VMEM((n - 1, heads, cols), jnp.bfloat16),
+            pltpu.VMEM((n - 1, heads, cols), jnp.bfloat16),
+            pltpu.VMEM((n // 2, heads, cols), jnp.float32),
+            pltpu.VMEM((2 * t, heads), jnp.float32),
+            pltpu.VMEM((n, 2 * groups, LANES), jnp.float32),
+            pltpu.VMEM((2, 8, cols), jnp.float32),
+            pltpu.VMEM((2, 8, LANES), jnp.float32),
+            dma((n,)), dma((n,)), dma((n,)), dma((n,)), dma((n,)), dma((n,)), dma((n,)), dma((n,)),
+            dma((2,)), dma((2,)),
+        ],
+        compiler_params=pltpu.CompilerParams(
+            collective_id=0, has_side_effects=True, vmem_limit_bytes=60 * 1024 * 1024
+        ),
+        cost_estimate=pl.CostEstimate(flops=flops, bytes_accessed=10 * t * width, transcendentals=0),
+    )(mask, cotangent, context, weight, row_stat.reshape(groups, LANES), col_stat.reshape(1, cols))
+    context_grad, update, row_new, col_new = out
+    return context_grad, update, row_new.reshape(heads), col_new.reshape(cols)
+
+
+def plain(context, cotangent, lengths, weight, row_stat, col_stat):
     data_groups = lax.axis_size("dp")
     seq_here = lengths.shape[0]
     target_len = cotangent.shape[0] // seq_here
@@ -45,6 +374,17 @@
     return (context_grad, update, row_new, col_new)
 
 
+def per_device(context, cotangent, lengths, weight, row_stat, col_stat):
+    n = lax.axis_size("dp")
+    heads, cols = weight.shape
+    tokens = 2 * cotangent.shape[0]
+    pairs = lax.axis_size("mp") == 2 and n >= 8 and n & (n - 1) == 0
+    whole_tiles = heads % (8 * LANES) == 0 and cols % LANES == 0 and tokens % TILE == 0
+    if pairs and whole_tiles:
+        return fused(n, context, cotangent, lengths, weight, row_stat, col_stat)
+    return plain(context, cotangent, lengths, weight, row_stat, col_stat)
+
+
 def solution(mesh):
     in_specs = (
         P("dp", "mp"),

time: 458 us -> 139 us (0.30)
  waiting for transfers between devices: 324 us -> 0 us
  Pallas kernels: 0 us -> 131 us
  blocking collectives: 74.6 us -> 0 us
  matrix products: 29.2 us -> 0 us
  between operations: 14.5 us -> 0.65 us
  other arithmetic: 11.2 us -> 0.01 us
    reduce_scatter x1 -> x0, waiting for transfers between devices: 177 us -> none  [per_device(): lax.psum_scatter(grad_term, 'dp', scatter_dimension=1, tiled=True)]
    all_gather x2 -> x0, waiting for transfers between devices: 147 us -> none  [the longest x1 107 us: per_device(): gathered = lax.all_gather(masked, 'mp', axis=0, tiled=True)]
    pallas_call x0 -> x1, Pallas kernels: none -> 131 us  [fused(): pl.pallas_call(functools.partial(kernel, n), out_shape=(jax.ShapeDtypeStr...]
    psum x3 -> x0, blocking collectives: 74.6 us -> none  [the longest x1 38.6 us: per_device(): square_sum = lax.psum(jnp.sum(raw_update * raw_update), ('dp', 'mp'))]
    dot_general x2 -> x0, matrix products: 29.2 us -> none  [the longest x1 14.7 us: per_device(): lax.dot_general(gathered, lax.all_gather(weight_b, 'dp', axis=1, tiled=Tr...]
  transfers between devices with their start and end apart: 3 -> 0, of which waited for: 3 -> 0; matrix products, arithmetic and copies ran while one was open for 1% -> 0% of each run, Pallas kernels for 0% -> 0%
where the time goes in v1:
time: 139 us
  Pallas kernels  131 us (94%)
  local copies, waits for them, and re-layouts  6.99 us (5%)
    pallas_call x1, Pallas kernels, fused(): pl.pallas_call(functools.partial(kernel, n), out_shape=(jax.ShapeDtypeStr...  131 us
    unnamed x10, local copies, waits for them, and re-layouts  5.31 us

profile of v1, /device:TPU:0, one launch (start us, length us, event | category | flops | bytes accessed | tf_op | source)
XLA Modules:
  0.0 138.9 jit_solution(12787959440169575643)
XLA Ops:
  0.6 0.7 lt.24
  1.4 0.1 lt.25
  1.4 0.1 lt.23
  1.5 0.8 broadcast_in_dim.2.mask_ref
  2.3 131.3 %shard_map.93 = (bf16[1024,1024]{1,0:T(8,128)(2,1)}, f32[1024,256]{1,0:T(8,128)}, f32[8,128]{1,0:T(8,128)}, f32[1,256]{1,0:T(1,128)}) custom-call(bf16[512,128]{1,0:T(8,128)(2,1)} %broadcast_in_dim.2.mask_ref, bf16[512,4096]{1,0:T(8,128)(2,1)} %cot_ref.1, bf16[1024,1024]{1,0:T(8,128)(2,1)} %ctx_ref.1, f32[1024,256]{1,0:T(8,128)} %w_ref.1, f32[8,128]{1,0:T(8,128)} %bitcast.8, ...), custom_call_target="tpu_custom_call" | custom-call | flops 17179869184 | bytes 20971520 | tf_op jit(solution)/shard_map/pallas_call | solution.py:306
  133.6 0.0 copy-start
  133.6 3.2 %copy.14 = bf16[1024,1024]{1,0:T(8,128)(2,1)} copy(bf16[1024,1024]{1,0:T(8,128)(2,1)} %get-tuple-element.16) | data formatting | bytes 4194304
  136.8 0.0 copy-done
  136.8 0.0 copy-start.1
  136.8 0.0 copy-start.2
  136.8 1.0 copy.15
  137.7 0.0 copy-done.1
  137.7 0.6 copy.16
  138.3 0.0 copy-done.2
  138.3 0.6 copy.17
  (2 shorter events, 0.0 us)
Async XLA Ops:
  133.6 3.2 %copy-start = (f32[1024,256]{1,0:T(8,128)S(1)}, f32[1024,256]{1,0:T(8,128)}, u32[]{:S(2)}) copy-start(f32[1024,256]{1,0:T(8,128)} %get-tuple-element.17) | copy-start | bytes 3145732
  136.8 1.0 copy-start.1
  136.8 1.6 %copy-start.2 = (f32[1,256]{1,0:T(1,128)S(1)}, f32[1,256]{1,0:T(1,128)}, u32[]{:S(2)}) copy-start(f32[1,256]{1,0:T(1,128)} %get-tuple-element.11) | copy-start | bytes 3076

commit v2 on v1

--- a/solution.py
+++ b/solution.py
@@ -10,7 +10,7 @@
 square_eps = 1e-30
 LANES = 128
 TILE = 256
-WINDOW = 3
+WINDOW = 4
 MESH = pl.DeviceIdType.MESH
 
 
@@ -44,14 +44,26 @@
     return order, after
 
 
+def weight_routes(n):
+    bits = [1 << k for k in range(n.bit_length() - 2, 0, -1)]
+    return bits + [1], bits[-1:] + bits[:-1] + [1]
+
+
+def onward(route, r):
+    used = [k for k, bit in enumerate(route) if r & bit]
+    return route[used[-1] + 1:] if used else route
+
+
 def weight_arrivals(n):
-    return sorted(range(2, n, 2), key=lambda r: (bin(r).count("1") + (n // low_bit(r, n)).bit_length(), r))
-
-
-def kernel(n, mask_ref, cot_ref, ctx_ref, w_ref, row_ref, col_ref,
+    pieces = [(r, h) for r in range(2, n, 2) for h in range(2)]
+    return sorted(pieces, key=lambda p: (bin(p[0]).count("1"), len(onward(weight_routes(n)[p[1]], p[0])) * -1, p[1]))
+
+
+def kernel(n, len_ref, cot_ref, ctx_ref, w_ref, row_ref, col_ref,
            cg_ref, up_ref, rown_ref, coln_ref,
-           ctx_t, g_all, w_all, inbox, outbox, kept, cg_acc, rv, cx, sx,
-           x_send, x_recv, w_send, w_recv, r_send, r_recv, v_send, v_recv, p_send, p_recv):
+           mask_ref, ctx_v, w_v, ctx_t, g_all, w_all, inbox, outbox, kept, cg_acc, rv, cx, sx,
+           x_send, x_recv, w_send, w_recv, r_send, r_recv, v_send, v_recv, p_send, p_recv,
+           b_sem, i_sem):
     me, mp = lax.axis_index("dp"), lax.axis_index("mp")
     other = 1 - mp
     t, width = cot_ref.shape
@@ -66,15 +78,34 @@
 
     order, after = schedule(n)
 
+    block_in = {}
+    for r in order:
+        columns = pl.ds(pl.multiple_of(flip(me, r) * cols, cols), cols)
+        block_in[r] = pltpu.make_async_copy(
+            cot_ref.at[:, columns], g_all.at[r, own_rows, :], b_sem.at[r])
+    w_in = pltpu.make_async_copy(w_ref, w_v, i_sem.at[0])
+    ctx_in = pltpu.make_async_copy(ctx_ref, ctx_v, i_sem.at[1])
+    for r in order[:WINDOW]:
+        block_in[r].start()
+    w_in.start()
+    for r in order[WINDOW:]:
+        block_in[r].start()
+    ctx_in.start()
+
+    seqs = len_ref.shape[0]
+    slots = t // seqs
+    position = lax.broadcasted_iota(jnp.int32, (slots, LANES), 0)
+    for q in range(seqs):
+        inside = jnp.where(position < len_ref[q], 1.0, 0.0)
+        mask_ref[q * slots:(q + 1) * slots, :] = inside.astype(jnp.bfloat16)
+
     def mask_block(r):
-        columns = pl.ds(pl.multiple_of(flip(me, r) * cols, cols), cols)
+        block_in[r].wait()
         m = mask_ref[...]
         m = jnp.concatenate([m] * (cols // LANES), axis=1)
-        g_all[r, own_rows, :] = cot_ref[:, columns] * m
-
-    w_all[0] = w_ref[...].astype(jnp.bfloat16)
-    for r in order[:WINDOW]:
-        mask_block(r)
+        g_all[r, own_rows, :] = g_all[r, own_rows, :] * m
+
+    mask_block(order[0])
     pl.semaphore_wait(barrier, n)
 
     x_copy = {}
@@ -92,35 +123,46 @@
         for r in order
     }
     for r in order[:WINDOW]:
+        if r != order[0]:
+            mask_block(r)
         x_copy[r].start()
+    w_in.wait()
+    w_all[0] = w_v[...].astype(jnp.bfloat16)
 
     w_copies = []
-
-    def weight_send(r):
-        bit = low_bit(r, n) // 2
-        while bit >= 1:
+    cut = heads * 5 // 8 // LANES * LANES
+    parts = (slice(0, cut), slice(cut, heads))
+
+    def weight_send(r, h):
+        for bit in onward(weight_routes(n)[h], r):
             copy = pltpu.make_async_remote_copy(
-                src_ref=w_all.at[r], dst_ref=w_all.at[r ^ bit],
-                send_sem=w_send.at[len(w_copies)], recv_sem=w_recv.at[r ^ bit],
+                src_ref=w_all.at[r, parts[h], :], dst_ref=w_all.at[r ^ bit, parts[h], :],
+                send_sem=w_send.at[len(w_copies)], recv_sem=w_recv.at[r ^ bit, h],
                 device_id=(flip(me, bit), mp), device_id_type=MESH)
             copy.start()
             w_copies.append(copy)
-            bit //= 2
-
-    def weight_wait(r):
+
+    w_seen = {(0, 0), (0, 1)}
+
+    def weight_wait(r, h):
+        if (r, h) in w_seen:
+            return
+        w_seen.add((r, h))
         pltpu.make_async_remote_copy(
-            src_ref=w_all.at[0], dst_ref=w_all.at[r],
-            send_sem=w_send.at[0], recv_sem=w_recv.at[r],
+            src_ref=w_all.at[0, parts[h], :], dst_ref=w_all.at[r, parts[h], :],
+            send_sem=w_send.at[0], recv_sem=w_recv.at[r, h],
             device_id=(flip(me, 1), mp), device_id_type=MESH).wait_recv()
 
-    weight_send(0)
+    weight_send(0, 0)
+    weight_send(0, 1)
     for r in order[WINDOW:]:
         mask_block(r)
 
     tokens = 2 * t
+    ctx_in.wait()
     for i in range(tokens // TILE):
         for j in range(heads // TILE):
-            ctx_t[j * TILE:(j + 1) * TILE, i * TILE:(i + 1) * TILE] = ctx_ref[
+            ctx_t[j * TILE:(j + 1) * TILE, i * TILE:(i + 1) * TILE] = ctx_v[
                 i * TILE:(i + 1) * TILE, j * TILE:(j + 1) * TILE].T
 
     def reduce_copy(r):
@@ -179,11 +221,10 @@
 
     arrivals = weight_arrivals(n)
     w_step = {}
-    for k, r in enumerate(arrivals):
-        w_step.setdefault(min(1 + (k * (n // 2 - 2)) // max(len(arrivals) - 1, 1), n - 1), []).append(r)
+    for k, piece in enumerate(arrivals):
+        w_step.setdefault(1 + k * (n // 2 - 1) // len(arrivals), []).append(piece)
     quarter = n // 4
     cg_step = {n // 2 + 1: 0, n // 2 + 3: 1, 3 * n // 4 + 1: 2}
-    w_seen = set(range(0, 1))
 
     for k, r in enumerate(order):
         x_in[r].wait_recv()
@@ -192,18 +233,16 @@
             x_copy[order[k + WINDOW]].start()
         weight_grad(r)
         for q in w_step.get(k, []):
-            weight_wait(q)
-            w_seen.add(q)
-            weight_send(q)
+            weight_wait(*q)
+            weight_send(*q)
         for q in order:
             if after.get(q) == k:
                 pass_on(q)
         if k in cg_step:
             blocks = order[cg_step[k] * quarter:(cg_step[k] + 1) * quarter]
             for q in blocks:
-                if q not in w_seen:
-                    weight_wait(q)
-                    w_seen.add(q)
+                weight_wait(q, 0)
+                weight_wait(q, 1)
             context_grad(blocks, cg_step[k] == 0, False)
 
     for q in incoming(0):
@@ -236,9 +275,8 @@
     col_copy.start()
     last = order[3 * quarter:]
     for q in last:
-        if q not in w_seen:
-            weight_wait(q)
-            w_seen.add(q)
+        weight_wait(q, 0)
+        weight_wait(q, 1)
     context_grad(last[:len(last) // 2], False, False)
     col_copy.wait_recv()
     col_new = decay_rate * col_ref[...] + (1.0 - decay_rate) * (
@@ -292,14 +330,28 @@
     s_copy.wait_send()
 
 
+def hand_on(*arrays):
+    steps = 4
+
+    def body(*refs):
+        for src, dst in zip(refs[:len(arrays)], refs[len(arrays):]):
+            dst[...] = src[...]
+
+    def spec(a):
+        if a.shape[0] % (16 * steps) == 0:
+            return pl.BlockSpec((a.shape[0] // steps, a.shape[1]), lambda i: (i, 0))
+        return pl.BlockSpec(a.shape, lambda i: (0, 0))
+
+    return pl.pallas_call(
+        body, grid=(steps,), in_specs=[spec(a) for a in arrays], out_specs=[spec(a) for a in arrays],
+        out_shape=[jax.ShapeDtypeStruct(a.shape, a.dtype) for a in arrays],
+    )(*arrays)
+
+
 def fused(n, context, cotangent, lengths, weight, row_stat, col_stat):
     t, width = cotangent.shape
     heads, cols = weight.shape
-    target_len = t // lengths.shape[0]
     groups = heads // LANES
-    inside = jnp.arange(target_len, dtype=jnp.int32)[None, :] < lengths[:, None]
-    mask = jnp.broadcast_to(inside[:, :, None], (lengths.shape[0], target_len, LANES))
-    mask = mask.astype(jnp.bfloat16).reshape(t, LANES)
     vmem = pl.BlockSpec(memory_space=pltpu.VMEM)
     dma = pltpu.SemaphoreType.DMA
     flops = 4 * 2 * t * heads * width
@@ -311,9 +363,12 @@
             jax.ShapeDtypeStruct((groups, LANES), jnp.float32),
             jax.ShapeDtypeStruct((1, cols), jnp.float32),
         ),
-        in_specs=[vmem] * 6,
+        in_specs=[pl.BlockSpec(memory_space=pltpu.SMEM)] + [pl.BlockSpec(memory_space=pl.ANY)] * 3 + [vmem] * 2,
         out_specs=(vmem,) * 4,
         scratch_shapes=[
+            pltpu.VMEM((t, LANES), jnp.bfloat16),
+            pltpu.VMEM((2 * t, heads), jnp.bfloat16),
+            pltpu.VMEM((heads, cols), jnp.float32),
             pltpu.VMEM((heads, 2 * t), jnp.bfloat16),
             pltpu.VMEM((n, 2 * t, cols), jnp.bfloat16),
             pltpu.VMEM((n, heads, cols), jnp.bfloat16),
@@ -324,15 +379,15 @@
             pltpu.VMEM((n, 2 * groups, LANES), jnp.float32),
             pltpu.VMEM((2, 8, cols), jnp.float32),
             pltpu.VMEM((2, 8, LANES), jnp.float32),
-            dma((n,)), dma((n,)), dma((n,)), dma((n,)), dma((n,)), dma((n,)), dma((n,)), dma((n,)),
-            dma((2,)), dma((2,)),
+            dma((n,)), dma((n,)), dma((2 * n,)), dma((n, 2)), dma((n,)), dma((n,)), dma((n,)), dma((n,)),
+            dma((2,)), dma((2,)), dma((n,)), dma((2,)),
         ],
         compiler_params=pltpu.CompilerParams(
             collective_id=0, has_side_effects=True, vmem_limit_bytes=60 * 1024 * 1024
         ),
         cost_estimate=pl.CostEstimate(flops=flops, bytes_accessed=10 * t * width, transcendentals=0),
-    )(mask, cotangent, context, weight, row_stat.reshape(groups, LANES), col_stat.reshape(1, cols))
-    context_grad, update, row_new, col_new = out
+    )(lengths, cotangent, context, weight, row_stat.reshape(groups, LANES), col_stat.reshape(1, cols))
+    context_grad, update, row_new, col_new = hand_on(*out)
     return context_grad, update, row_new.reshape(heads), col_new.reshape(cols)
 
 

time: 139 us -> 122 us (0.88)
  Pallas kernels: 131 us -> 121 us
  local copies, waits for them, and re-layouts: 6.99 us -> 0 us
    pallas_call x1, Pallas kernels: 131 us -> 117 us  [fused(): pl.pallas_call(functools.partial(kernel, n), out_shape=(jax.ShapeDtypeStr...]
    unnamed x10 -> x0, local copies, waits for them, and re-layouts: 5.31 us -> none
    pallas_call x0 -> x1, Pallas kernels: none -> 4.15 us  [hand_on(): pl.pallas_call(body, grid=(steps,), in_specs=[spec(a) for a in arrays], o...]
where the time goes in v2:
time: 122 us
  Pallas kernels  121 us (99%)
    pallas_call x1, Pallas kernels, fused(): pl.pallas_call(functools.partial(kernel, n), out_shape=(jax.ShapeDtypeStr...  117 us
    pallas_call x1, Pallas kernels, hand_on(): pl.pallas_call(body, grid=(steps,), in_specs=[spec(a) for a in arrays], o...  4.15 us

profile of v2, /device:TPU:0, one launch (start us, length us, event | category | flops | bytes accessed | tf_op | source)
XLA Modules:
  0.0 121.6 jit_solution(5711016305300542025)
XLA Ops:
  0.6 116.8 %shard_map.93 = (bf16[1024,1024]{1,0:T(8,128)(2,1)}, f32[1024,256]{1,0:T(8,128)}, f32[8,128]{1,0:T(8,128)}, f32[1,256]{1,0:T(1,128)}) custom-call(s32[16]{0:T(128)} %len_ref.1, bf16[512,4096]{1,0:T(8,128)(2,1)} %cot_ref.1, bf16[1024,1024]{1,0:T(8,128)(2,1)} %ctx_ref.1, f32[1024,256]{1,0:T(8,128)} %w_ref.1, f32[8,128]{1,0:T(8,128)} %bitcast.4, f32[1,256]{1,0:T(1,128)} %bitcast.6), custom_call_target="tpu_custom_call" | custom-call | flops 17179869184 | bytes 20971520 | tf_op jit(solution)/shard_map/pallas_call | solution.py:358
  117.5 4.2 %shard_map.94 = (bf16[1024,1024]{1,0:T(8,128)(2,1)}, f32[1024,256]{1,0:T(8,128)}, f32[8,128]{1,0:T(8,128)}, f32[1,256]{1,0:T(1,128)}) custom-call(bf16[1024,1024]{1,0:T(8,128)(2,1)} %get-tuple-element.12.refs_0_, f32[1024,256]{1,0:T(8,128)} %get-tuple-element.13.refs_1_, f32[8,128]{1,0:T(8,128)} %get-tuple-element.14.refs_2_, f32[1,256]{1,0:T(1,128)} %get-tuple-element.15.refs_3_), custom_call_target="tpu_custom_call" | custom-call | tf_op jit(solution)/shard_map/pallas_call | solution.py:345

commit v3 on v2

--- a/solution.py
+++ b/solution.py
@@ -61,7 +61,7 @@
 
 def kernel(n, len_ref, cot_ref, ctx_ref, w_ref, row_ref, col_ref,
            cg_ref, up_ref, rown_ref, coln_ref,
-           mask_ref, ctx_v, w_v, ctx_t, g_all, w_all, inbox, outbox, kept, cg_acc, rv, cx, sx,
+           cg_v, mask_ref, ctx_v, w_v, ctx_t, g_all, w_all, inbox, outbox, kept, cg_acc, rv, cx, sx,
            x_send, x_recv, w_send, w_recv, r_send, r_recv, v_send, v_recv, p_send, p_recv,
            b_sem, i_sem):
     me, mp = lax.axis_index("dp"), lax.axis_index("mp")
@@ -215,7 +215,7 @@
                                        preferred_element_type=jnp.float32)
                 total = term if total is None else total + term
             if last:
-                cg_ref[rows, :] = total.astype(jnp.bfloat16)
+                cg_v[rows, :] = total.astype(jnp.bfloat16)
             else:
                 cg_acc[rows, :] = total
 
@@ -244,6 +244,12 @@
                 weight_wait(q, 0)
                 weight_wait(q, 1)
             context_grad(blocks, cg_step[k] == 0, False)
+        if k == n - 2:
+            blocks = order[3 * quarter:n - 2]
+            for q in blocks + order[n - 2:]:
+                weight_wait(q, 0)
+                weight_wait(q, 1)
+            context_grad(blocks, False, False)
 
     for q in incoming(0):
         r_copy[q].wait_recv()
@@ -273,11 +279,8 @@
         src_ref=cx.at[0], dst_ref=cx.at[1], send_sem=p_send.at[0], recv_sem=p_recv.at[0],
         device_id=(me, other), device_id_type=MESH)
     col_copy.start()
-    last = order[3 * quarter:]
-    for q in last:
-        weight_wait(q, 0)
-        weight_wait(q, 1)
-    context_grad(last[:len(last) // 2], False, False)
+    last = order[n - 2:]
+    context_grad(last[:1], False, False)
     col_copy.wait_recv()
     col_new = decay_rate * col_ref[...] + (1.0 - decay_rate) * (
         (cx[0, 0:1, :] + cx[1, 0:1, :]) / (2 * heads))
@@ -293,7 +296,9 @@
             device_id=(flip(me, q), mp), device_id_type=MESH)
         copy.start()
         v_copy.append(copy)
-    context_grad(last[len(last) // 2:], False, True)
+    context_grad(last[-1:], False, True)
+    cg_out = pltpu.make_async_copy(cg_v, cg_ref, i_sem.at[2])
+    cg_out.start()
     for copy in v_copy:
         copy.wait_recv()
     sums = [rv[q] for q in range(n)]
@@ -328,23 +333,38 @@
     for copy in v_copy:
         copy.wait_send()
     s_copy.wait_send()
+    cg_out.wait()
 
 
 def hand_on(*arrays):
-    steps = 4
+    pieces = []
+    for k, a in enumerate(arrays):
+        size = 128 if a.shape[0] % 128 == 0 else a.shape[0]
+        pieces += [(k, slice(i, i + size)) for i in range(0, a.shape[0], size)]
+    count = len(arrays)
 
     def body(*refs):
-        for src, dst in zip(refs[:len(arrays)], refs[len(arrays):]):
-            dst[...] = src[...]
-
-    def spec(a):
-        if a.shape[0] % (16 * steps) == 0:
-            return pl.BlockSpec((a.shape[0] // steps, a.shape[1]), lambda i: (i, 0))
-        return pl.BlockSpec(a.shape, lambda i: (0, 0))
-
+        src, dst, held = refs[:count], refs[count:2 * count], refs[2 * count:3 * count]
+        sem_in, sem_out = refs[3 * count:]
+        into = [pltpu.make_async_copy(src[k].at[rows, :], held[k].at[rows, :], sem_in.at[i])
+                for i, (k, rows) in enumerate(pieces)]
+        out = [pltpu.make_async_copy(held[k].at[rows, :], dst[k].at[rows, :], sem_out.at[i])
+               for i, (k, rows) in enumerate(pieces)]
+        for copy in into:
+            copy.start()
+        for first, second in zip(into, out):
+            first.wait()
+            second.start()
+        for copy in out:
+            copy.wait()
+
+    anywhere = pl.BlockSpec(memory_space=pl.ANY)
     return pl.pallas_call(
-        body, grid=(steps,), in_specs=[spec(a) for a in arrays], out_specs=[spec(a) for a in arrays],
+        body, in_specs=[anywhere] * count, out_specs=[anywhere] * count,
         out_shape=[jax.ShapeDtypeStruct(a.shape, a.dtype) for a in arrays],
+        scratch_shapes=[pltpu.VMEM(a.shape, a.dtype) for a in arrays]
+        + [pltpu.SemaphoreType.DMA((len(pieces),)), pltpu.SemaphoreType.DMA((len(pieces),))],
+        compiler_params=pltpu.CompilerParams(vmem_limit_bytes=60 * 1024 * 1024),
     )(*arrays)
 
 
@@ -364,8 +384,9 @@
             jax.ShapeDtypeStruct((1, cols), jnp.float32),
         ),
         in_specs=[pl.BlockSpec(memory_space=pltpu.SMEM)] + [pl.BlockSpec(memory_space=pl.ANY)] * 3 + [vmem] * 2,
-        out_specs=(vmem,) * 4,
+        out_specs=(pl.BlockSpec(memory_space=pl.ANY),) + (vmem,) * 3,
         scratch_shapes=[
+            pltpu.VMEM((2 * t, heads), jnp.bfloat16),
             pltpu.VMEM((t, LANES), jnp.bfloat16),
             pltpu.VMEM((2 * t, heads), jnp.bfloat16),
             pltpu.VMEM((heads, cols), jnp.float32),
@@ -380,7 +401,7 @@
             pltpu.VMEM((2, 8, cols), jnp.float32),
             pltpu.VMEM((2, 8, LANES), jnp.float32),
             dma((n,)), dma((n,)), dma((2 * n,)), dma((n, 2)), dma((n,)), dma((n,)), dma((n,)), dma((n,)),
-            dma((2,)), dma((2,)), dma((n,)), dma((2,)),
+            dma((2,)), dma((2,)), dma((n,)), dma((3,)),
         ],
         compiler_params=pltpu.CompilerParams(
             collective_id=0, has_side_effects=True, vmem_limit_bytes=60 * 1024 * 1024

time: 122 us -> 120 us (0.984)
  Pallas kernels: 121 us -> 119 us
    pallas_call x1, Pallas kernels: 4.15 us -> 2.92 us  [hand_on(): pl.pallas_call(body, in_specs=[anywhere] * count, out_specs=[anywhere] *...]
where the time goes in v3:
time: 120 us
  Pallas kernels  119 us (99%)
    pallas_call x1, Pallas kernels, fused(): pl.pallas_call(functools.partial(kernel, n), out_shape=(jax.ShapeDtypeStr...  116 us
    pallas_call x1, Pallas kernels, hand_on(): pl.pallas_call(body, in_specs=[anywhere] * count, out_specs=[anywhere] *...  2.92 us

profile of v3, /device:TPU:0, one launch (start us, length us, event | category | flops | bytes accessed | tf_op | source)
XLA Modules:
  0.0 119.6 jit_solution(11083047961485036562)
XLA Ops:
  0.6 116.0 %shard_map.93 = (bf16[1024,1024]{1,0:T(8,128)(2,1)}, f32[1024,256]{1,0:T(8,128)}, f32[8,128]{1,0:T(8,128)}, f32[1,256]{1,0:T(1,128)}) custom-call(s32[16]{0:T(128)} %len_ref.1, bf16[512,4096]{1,0:T(8,128)(2,1)} %cot_ref.1, bf16[1024,1024]{1,0:T(8,128)(2,1)} %ctx_ref.1, f32[1024,256]{1,0:T(8,128)} %w_ref.1, f32[8,128]{1,0:T(8,128)} %bitcast.4, f32[1,256]{1,0:T(1,128)} %bitcast.6), custom_call_target="tpu_custom_call" | custom-call | flops 17179869184 | bytes 20971520 | tf_op jit(solution)/shard_map/pallas_call | solution.py:378
  116.7 2.9 %shard_map.94 = (bf16[1024,1024]{1,0:T(8,128)(2,1)}, f32[1024,256]{1,0:T(8,128)}, f32[8,128]{1,0:T(8,128)}, f32[1,256]{1,0:T(1,128)}) custom-call(bf16[1024,1024]{1,0:T(8,128)(2,1)} %get-tuple-element.12.refs_0_, f32[1024,256]{1,0:T(8,128)} %get-tuple-element.13.refs_1_, f32[8,128]{1,0:T(8,128)} %get-tuple-element.14.refs_2_, f32[1,256]{1,0:T(1,128)} %get-tuple-element.15.refs_3_), custom_call_target="tpu_custom_call" | custom-call | tf_op jit(solution)/shard_map/pallas_call | solution.py:362
